TPU v7x, 128 devices: a whole 4x4x4 slice. The times are simulated.
128 devices in a mesh: dp: 16 (over x, y_hi, core), tensor: 8 (over z, y_lo).
Axes of the slice: x: 4, y: 4 (y_hi: 2, y_lo: 2; y = y_hi * 2 + y_lo), z: 4, core: 2. Of those that a mesh axis runs over, the one named last changes fastest.
Arguments:
- context: bfloat16 [16384, 6144], P('dp', 'tensor'), may hold values from -6 to 6
- cotangent: bfloat16 [16384, 6144], P(('dp', 'tensor')), may hold values from -24 to 24
- weight: bfloat16 [6144, 6144], P(None, 'tensor'), may hold values from -49 to 49
- first_moment: float32 [6144, 6144], P('dp', 'tensor'), may hold values from -49 to 49
- second_moment: float32 [6144, 6144], P('dp', 'tensor'), may hold values from 0.25 to 4
Outputs:
- context_grad: bfloat16 [16384, 6144], P('dp', 'tensor')
- momentum: float32 [6144, 6144], P('dp', 'tensor')
- variance: float32 [6144, 6144], P('dp', 'tensor')
- lamb_step: float32 [6144, 6144], P('dp', 'tensor')
All inputs are finite; a program needn't handle non-finite values.
Results may differ from a plain program's by a relative error of at most 0.0065.
Values may be sent and summed in bfloat16 or wider, within the bound.
A program may use at most 192 MiB of HBM per device.

v0:
```python
import math

import jax
import jax.numpy as jnp
from jax import lax
from jax.sharding import PartitionSpec as P

HEADS = 48
HD = 128


def shards(context, cotangent, weight, first_moment, second_moment):
    multiplier = 1.0 / math.sqrt(HEADS * HD)
    shard_rows = first_moment.shape[0]
    row_start = lax.axis_index("dp") * shard_rows
    weight_part = lax.dynamic_slice_in_dim(weight, row_start, shard_rows, 0).astype(jnp.float32)
    weight_local = jnp.sum(weight_part * weight_part)
    gathered = lax.all_gather(cotangent, "tensor", axis=0, tiled=True)
    context_grad = (
        jnp.dot(gathered, weight, preferred_element_type=jnp.float32) * multiplier
    ).astype(jnp.bfloat16)
    product = lax.dot_general(
        gathered, context, (((0,), (0,)), ((), ())), preferred_element_type=jnp.float32
    )
    grad = lax.psum_scatter(
        (product * multiplier).astype(jnp.bfloat16), "dp", scatter_dimension=0, tiled=True
    ).astype(jnp.float32)
    momentum = 0.9 * first_moment + 0.1 * grad
    variance = 0.95 * second_moment + 0.05 * grad * grad
    update = momentum / (jnp.sqrt(variance) + 1e-06) + 0.1 * weight_part
    update_local = jnp.sum(update * update)
    weight_total, update_total = lax.psum((weight_local, update_local), ("dp", "tensor"))
    lamb_step = jnp.sqrt(weight_total) / jnp.sqrt(update_total + 1e-06) * update
    return (context_grad, momentum, variance, lamb_step)


def solution(mesh):
    in_specs = (
        P("dp", "tensor"),
        P(("dp", "tensor"), None),
        P(None, "tensor"),
        P("dp", "tensor"),
        P("dp", "tensor"),
    )
    out_specs = (P("dp", "tensor"), P("dp", "tensor"), P("dp", "tensor"), P("dp", "tensor"))
    return jax.shard_map(shards, mesh=mesh, in_specs=in_specs, out_specs=out_specs, check_vma=False)
```

profile of v0, /device:TPU:1, one launch (start us, length us, event | category | flops | bytes accessed | tf_op | source)
XLA Modules:
  0.0 464.7 jit_solution(17228368551530913026)
XLA Ops:
  7.2 0.0 copy-start
  7.2 0.0 all-gather.2.cloned.1.call-start
  7.2 0.7 all-gather.2.cloned.1.call-update
  7.9 0.0 reduce-scatter.2.cloned.1.call-start
  8.0 251.9 %all-gather.2.cloned.1.call-done = bf16[1024,6144]{1,0:T(8,128)(2,1)} async-done(((bf16[128,6144]{1,0:T(8,128)(2,1)}), bf16[1024,6144]{1,0:T(8,128)(2,1)}) %all-gather.2.cloned.1.call-update) | async-done | bytes 12582928 | tf_op jit(solution)/shard_map/all_gather | solution.py:18
  259.9 0.0 copy-done
  259.9 17.4 %multiply_convert_fusion = bf16[6144,768]{1,0:T(8,128)(2,1)} fusion(bf16[1024,6144]{1,0:T(8,128)(2,1)} %all-gather.2.cloned.1.call-done, bf16[1024,768]{1,0:T(8,128)(2,1)S(1)} %copy-done), kind=kOutput, calls=%fused_computation | convolution fusion | flops 9673113600 | bytes 23592960 | tf_op jit(solution)/shard_map/dot_general | solution.py:22
  277.3 0.0 reduce-scatter.2.cloned.1.call-update
  277.3 16.5 %multiply_convert_fusion.1 = bf16[1024,768]{1,0:T(8,128)(2,1)} fusion(bf16[1024,6144]{1,0:T(8,128)(2,1)} %all-gather.2.cloned.1.call-done, bf16[6144,768]{1,0:T(8,128)(2,1)} %param.7), kind=kOutput, calls=%fused_computation.1 | convolution fusion | flops 9665249280 | bytes 23592960 | tf_op jit(solution)/shard_map/dot_general | solution.py:20
  293.8 91.0 %reduce-scatter.2.cloned.1.call-done = bf16[384,768]{1,0:T(8,128)(2,1)} async-done(((bf16[6144,768]{1,0:T(8,128)(2,1)}), bf16[384,768]{1,0:T(8,128)(2,1)}) %reduce-scatter.2.cloned.1.call-update) | async-done | bytes 589840 | tf_op jit(solution)/shard_map/reduce_scatter | solution.py:25
  384.7 5.0 %multiply_reduce_fusion = (f32[]{:T(128)}, f32[384,768]{1,0:T(8,128)S(1)}, f32[384,768]{1,0:T(8,128)}, f32[384,768]{1,0:T(8,128)}, f32[]{:T(128)}) fusion(bf16[6144,768]{1,0:T(8,128)(2,1)} %param.7, s32[]{:T(128)S(6)} %select_n.3, bf16[384,768]{1,0:T(8,128)(2,1)} %reduce-scatter.2.cloned.1.call-done, f32[384,768]{1,0:T(8,128)} %param.9, f32[384,768]{1,0:T(8,128)} %param.8), kind=kLoop, calls=%fused_computation.10 | loop fusion | flops 5013502 | bytes 7077900 | tf_op jit(solution)/shard_map/reduce_sum | solution.py:31
  389.8 65.7 %all-reduce = (f32[]{:T(128)}, f32[]{:T(128)}) all-reduce(f32[]{:T(128)} %get-tuple-element.10, f32[]{:T(128)} %get-tuple-element.6), channel_id=1, replica_groups=mesh['dp'=16,'tensor'=8] {'dp','tensor'}, use_global_device_ids=true, to_apply=%region_2.0 | all-reduce | flops 2 | bytes 16 | tf_op jit(solution)/shard_map/psum | solution.py:32
  456.7 1.1 broadcast_multiply_fusion
Async XLA Ops:
  7.2 252.7 %copy-start = (bf16[1024,768]{1,0:T(8,128)(2,1)S(1)}, bf16[1024,768]{1,0:T(8,128)(2,1)}, u32[]{:S(2)}) copy-start(bf16[1024,768]{1,0:T(8,128)(2,1)} %param.5) | copy-start | bytes 4718596
  7.2 252.7 %all-gather.2.cloned.1.call-start = ((), (), s32[]{:S(2)}) async-start(), calls=%async_computation.1 | async-start | bytes 14155776 | tf_op jit(solution)/shard_map/all_gather | solution.py:18
  7.9 376.8 %reduce-scatter.2.cloned.1.call-start = ((), (), s32[]{:S(2)}) async-start(), calls=%async_computation.2 | async-start | bytes 10027008 | tf_op jit(solution)/shard_map/reduce_scatter | solution.py:25
Sparse Core Ops, SparseCore 0:
  9.7 250.1 all-gather.1
  277.4 107.2 reduce-scatter.1
where the time goes:
time: 465 us
  waiting for transfers between devices  344 us (74%)
  blocking collectives  65.7 us (14%)
  matrix products  33.9 us (7%)
  between operations  15.3 us (3%)
  other arithmetic  6.1 us (1%)
    all_gather x1, waiting for transfers between devices, shards(): gathered = lax.all_gather(cotangent, 'tensor', axis=0, tiled=True)  252 us
    reduce_scatter x1, waiting for transfers between devices, shards(): lax.psum_scatter((product * multiplier).astype(jnp.bfloat16), 'dp', scatt...  91 us
    psum x1, blocking collectives, shards(): lax.psum((weight_local, update_local), ('dp', 'tensor'))  65.7 us
    dot_general x1, matrix products, shards(): lax.dot_general(gathered, context, (((0,), (0,)), ((), ())), preferred_el...  17.4 us
    dot_general x1, matrix products, shards(): jnp.dot(gathered, weight, preferred_element_type=jnp.float32) * multiplier  16.5 us
  transfers between devices with their start and end apart: 2, of which 2 were waited for; matrix products, arithmetic and copies ran while one was open for 4% of the time, Pallas kernels for 0%

commit v1 on v0

v1 whole, which is shorter than its diff:
```python
import functools
import math

import jax
import jax.numpy as jnp
from jax import lax
from jax.experimental import pallas as pl
from jax.experimental.pallas import tpu as pltpu
from jax.sharding import PartitionSpec as P

HEADS = 48
HD = 128
MESH = pl.DeviceIdType.MESH
PARTS = 8
F32 = jnp.float32
BF16 = jnp.bfloat16

MESSAGES = (
    ("z+", 0, 0, 0, 128),
    ("z-", 0, 0, 0, 128),
    ("y", 0, 0, 0, 128),
    ("z+", 0, 1, 0, 80),
    ("z-", 0, 1, 0, 80),
    ("z+", 3, 0, 0, 64),
    ("z-", 1, 0, 64, 128),
    ("y", 3, 0, 80, 128),
    ("y", 1, 0, 80, 128),
    ("z+", 3, 1, 0, 48),
    ("z-", 1, 1, 48, 80),
    ("y", 2, 0, 80, 128),
)


def kernel(
    multiplier,
    cot, ctx, weight, first, second,
    cg_out, mo_out, va_out, la_out,
    gath, wv, cx, cxt, prod, cr, xr, ys, yr, acc, cgb, mb, vb, up, base, one, two,
    own_sem, w_sem, in_sem, out_sem, gs, gr, ds_, dr, xs_, xr_, ysem, s1, r1, s2, r2,
):
    d, t = lax.axis_index("dp"), lax.axis_index("tensor")
    x, yh, c = d // 4, (d // 2) % 2, d % 2
    z, yl = t // 2, t % 2
    half = gath.shape[2] // 2
    rows = cot.shape[0]

    def device(x, yh, c, z, yl):
        return ((x * 2 + yh) * 2 + c, z * 2 + yl)

    links = {
        "z+": device(x, yh, c, (z + 1) % 4, yl),
        "z-": device(x, yh, c, (z + 3) % 4, yl),
        "y": device(x, yh, c, z, 1 - yl),
    }
    sibling = device(x, yh, 1 - c, z, yl)

    def offset(s, h):
        r = s % 4
        return ((2 + 3 * r + 3 * (r * (r - 1) // 2)) * (1 + 2 * h)) % 4

    def owner(s, h):
        oy = (yh + 1 - s // 4) % 2
        return (((x + offset(s, h)) % 4) * 2 + oy) * 2 + h

    def own_copy(s, h):
        at = pl.multiple_of(owner(s, h) * half, 128)
        return pltpu.make_async_copy(
            cot.at[:, pl.ds(at, half)],
            gath.at[s, pl.ds(pl.multiple_of(t * rows, rows), rows), pl.ds(h * half, half)],
            own_sem.at[s, h],
        )

    def w_copy(s, h):
        at = pl.multiple_of(owner(s, h) * half, 128)
        return pltpu.make_async_copy(
            weight.at[pl.ds(at, half)], wv.at[s, pl.ds(h * half, half)], w_sem.at[s, h]
        )

    ctx_copy = pltpu.make_async_copy(ctx, cx, in_sem.at[0])
    first_copy = pltpu.make_async_copy(first, mb, in_sem.at[1])
    second_copy = pltpu.make_async_copy(second, vb, in_sem.at[2])

    def message(s, k, received):
        link, dz, yb, lo, hi = MESSAGES[k]
        if received:
            dz = (dz + {"z+": 3, "z-": 1, "y": 0}[link]) % 4
            yb = 1 - yb if link == "y" else yb
        block = ((z + dz) % 4) * 2 + (1 - yl if yb else yl)
        ref = gath.at[s, pl.ds(pl.multiple_of(block * rows + lo, 16), hi - lo)]
        return pltpu.make_async_remote_copy(
            src_ref=ref, dst_ref=ref, send_sem=gs.at[s, k], recv_sem=gr.at[s, k],
            device_id=links[link], device_id_type=MESH,
        )

    def send(s, *ks):
        for k in ks:
            message(s, k, False).start()

    def arrive(s, *ks):
        for k in ks:
            message(s, k, True).wait_recv()

    def stage_a(s):
        for h in range(2):
            own_copy(s, h).wait()
        send(s, 0, 1, 2)

    def stage_b(s):
        arrive(s, 2)
        send(s, 3, 4)
        arrive(s, 0)
        send(s, 5, 7)
        arrive(s, 1)
        send(s, 6, 8)

    def stage_c(s):
        arrive(s, 3)
        send(s, 9)
        arrive(s, 4)
        send(s, 10)
        arrive(s, 6)
        send(s, 11)

    def core_copy(s):
        return pltpu.make_async_remote_copy(
            src_ref=prod.at[s, 1 - c], dst_ref=cr.at[s], send_sem=ds_.at[s], recv_sem=dr.at[s],
            device_id=sibling, device_id_type=MESH,
        )

    def x_copy(s):
        dx = offset(s, c)
        slot = (1 - s // 4) * 3 + (dx + 3) % 4
        return pltpu.make_async_remote_copy(
            src_ref=prod.at[s, c], dst_ref=xr.at[slot], send_sem=xs_.at[s], recv_sem=xr_.at[slot],
            device_id=device((x + dx) % 4, yh, c, z, yl), device_id_type=MESH,
        )

    def x_arrive(slot):
        pltpu.make_async_remote_copy(
            src_ref=xr.at[slot], dst_ref=xr.at[slot], send_sem=xs_.at[0], recv_sem=xr_.at[slot],
            device_id=sibling, device_id_type=MESH,
        ).wait_recv()

    y_copy = pltpu.make_async_remote_copy(
        src_ref=ys, dst_ref=yr, send_sem=ysem.at[0], recv_sem=ysem.at[1],
        device_id=device(x, 1 - yh, c, z, yl), device_id_type=MESH,
    )

    group1 = [
        ((x + dx) % 4, (c + dc) % 2, (dx * 2 + dc)) for dx in range(4) for dc in range(2) if dx or dc
    ]
    y = yh * 2 + yl
    group2 = [
        ((y + dy) % 4, (z + dz) % 4, (dy * 4 + dz)) for dy in range(4) for dz in range(4) if dy or dz
    ]

    def one_copy(px, pc, slot):
        return pltpu.make_async_remote_copy(
            src_ref=one.at[0], dst_ref=one.at[slot], send_sem=s1.at[slot], recv_sem=r1.at[slot],
            device_id=device(px, yh, pc, z, yl), device_id_type=MESH,
        )

    def two_copy(py, pz, slot):
        return pltpu.make_async_remote_copy(
            src_ref=two.at[0], dst_ref=two.at[slot], send_sem=s2.at[slot], recv_sem=r2.at[slot],
            device_id=device(x, py // 2, c, pz, py % 2), device_id_type=MESH,
        )

    for s in range(PARTS):
        for h in range(2):
            own_copy(s, h).start()
        if s == 0:
            ctx_copy.start()
    for s in range(PARTS):
        for h in range(2):
            w_copy(s, h).start()
    first_copy.start()
    second_copy.start()

    barrier = pltpu.get_barrier_semaphore()
    for px, pc, _ in group1:
        pl.semaphore_signal(barrier, inc=1, device_id=device(px, yh, pc, z, yl), device_id_type=MESH)
    for py, pz, _ in group2:
        pl.semaphore_signal(barrier, inc=1, device_id=device(x, py // 2, c, pz, py % 2), device_id_type=MESH)
    pl.semaphore_wait(barrier, len(group1) + len(group2))

    stage_a(0)
    ctx_copy.wait()
    for k in range(cx.shape[0] // 128):
        cxt[:, k * 128 : (k + 1) * 128] = cx[k * 128 : (k + 1) * 128, :].T

    def product(s):
        for n in range(2 * half // 256):
            value = jnp.dot(cxt[...], gath[s, :, n * 256 : (n + 1) * 256], preferred_element_type=F32)
            value = (value * multiplier).astype(BF16)
            for k in range(2):
                column = n * 256 + k * 128
                prod[s, column // half, :, column % half : column % half + 128] = value[:, k * 128 : (k + 1) * 128]

    def context_part(s, last):
        for h in range(2):
            w_copy(s, h).wait()

        @pl.loop(0, acc.shape[1] // 256)
        def _(n):
            cols = pl.ds(pl.multiple_of(n * 256, 256), 256)
            value = jnp.dot(gath[s], wv[s, :, cols], preferred_element_type=F32)
            if last:
                cgb[:, cols] = ((acc[:, cols] + value) * multiplier).astype(BF16)
            else:
                acc[:, cols] += value

    def whole(s):
        arrive(s, 5, 7, 8, 9, 10, 11)
        product(s)
        core_copy(s).start()

    acc[...] = jnp.zeros_like(acc)

    @pl.loop(0, PARTS + 1)
    def _(i):
        @pl.when(i < PARTS - 1)
        def _():
            stage_a(i + 1)

        @pl.when(i < PARTS)
        def _():
            stage_b(i)

        @pl.when(i > 0)
        def _():
            stage_c(i - 1)

        @pl.when(i > 1)
        def _():
            s = i - 2
            whole(s)
            context_part(s, False)
            core_copy(s).wait_recv()

            @pl.when(s % 4 != 3)
            def _():
                prod[s, c] = (prod[s, c].astype(F32) + cr[s].astype(F32)).astype(BF16)
                x_copy(s).start()

            @pl.when(s == 3)
            def _():
                for slot in range(3, 6):
                    x_arrive(slot)
                total = prod[s, c].astype(F32) + cr[s].astype(F32)
                for slot in range(3, 6):
                    total += xr[slot].astype(F32)
                ys[...] = total.astype(BF16)
                y_copy.start()

    s = PARTS - 1
    whole(s)
    y_copy.wait_recv()
    base[...] = yr[...].astype(F32)
    for slot in range(3):
        x_arrive(slot)
        base[...] += xr[slot].astype(F32)
    context_part(s, True)
    cg_copy = pltpu.make_async_copy(cgb, cg_out, out_sem.at[0])
    cg_copy.start()
    first_copy.wait()
    second_copy.wait()
    core_copy(s).wait_recv()

    def fold(value):
        total = value[0:8, 0:128]
        for r in range(value.shape[0] // 8):
            for k in range(value.shape[1] // 128):
                if r or k:
                    total += value[r * 8 : (r + 1) * 8, k * 128 : (k + 1) * 128]
        return total

    zero = jnp.zeros((8, 128), F32)
    u_sum, w_sum = zero, zero
    for k in range(half // 128):
        cols = slice(k * 128, (k + 1) * 128)
        g = (base[:, cols] + prod[s, c, :, cols].astype(F32) + cr[s, :, cols].astype(F32)).T
        w = wv[s, pl.ds(pl.multiple_of(c * half + k * 128, 128), 128), :].astype(F32)
        m = 0.9 * mb[cols, :] + 0.1 * g
        v = 0.95 * vb[cols, :] + 0.05 * g * g
        u = m / (jnp.sqrt(v) + 1e-06) + 0.1 * w
        mb[cols, :] = m
        vb[cols, :] = v
        up[cols, :] = u
        u_sum += fold(u * u)
        w_sum += fold(w * w)
    one[0, 0:8] = u_sum
    one[0, 8:16] = w_sum
    for px, pc, slot in group1:
        one_copy(px, pc, slot).start()
    mo_copy = pltpu.make_async_copy(mb, mo_out, out_sem.at[1])
    va_copy = pltpu.make_async_copy(vb, va_out, out_sem.at[2])
    mo_copy.start()
    va_copy.start()
    for px, pc, slot in group1:
        one_copy(px, pc, slot).wait_recv()
    total = one[0]
    for _, _, slot in group1:
        total += one[slot]
    two[0] = total
    for py, pz, slot in group2:
        two_copy(py, pz, slot).start()
    for py, pz, slot in group2:
        two_copy(py, pz, slot).wait_recv()
    total = two[0]
    for _, _, slot in group2:
        total += two[slot]
    u_total = jnp.sum(total[0:8], keepdims=True)
    w_total = jnp.sum(total[8:16], keepdims=True)
    up[...] = up[...] * (jnp.sqrt(w_total) / jnp.sqrt(u_total + 1e-06))
    la_copy = pltpu.make_async_copy(up, la_out, out_sem.at[3])
    la_copy.start()

    @pl.loop(0, PARTS)
    def _(s):
        for k in range(len(MESSAGES)):
            message(s, k, False).wait_send()
        core_copy(s).wait_send()

        @pl.when(s % 4 != 3)
        def _():
            x_copy(s).wait_send()

    y_copy.wait_send()
    for px, pc, slot in group1:
        one_copy(px, pc, slot).wait_send()
    for py, pz, slot in group2:
        two_copy(py, pz, slot).wait_send()
    cg_copy.wait()
    mo_copy.wait()
    va_copy.wait()
    la_copy.wait()


def shards(context, cotangent, weight, first_moment, second_moment):
    multiplier = 1.0 / math.sqrt(HEADS * HD)
    tokens, inner = context.shape
    rows, model = cotangent.shape
    part = model // PARTS
    half = part // 2
    sem = pltpu.SemaphoreType.DMA
    n = len(MESSAGES)
    scratch = [
        pltpu.VMEM((PARTS, tokens, part), BF16),
        pltpu.VMEM((PARTS, part, inner), BF16),
        pltpu.VMEM((tokens, inner), BF16),
        pltpu.VMEM((inner, tokens), BF16),
        pltpu.VMEM((PARTS, 2, inner, half), BF16),
        pltpu.VMEM((PARTS, inner, half), BF16),
        pltpu.VMEM((6, inner, half), BF16),
        pltpu.VMEM((inner, half), BF16),
        pltpu.VMEM((inner, half), BF16),
        pltpu.VMEM((tokens, inner), F32),
        pltpu.VMEM((tokens, inner), BF16),
        pltpu.VMEM((half, inner), F32),
        pltpu.VMEM((half, inner), F32),
        pltpu.VMEM((half, inner), F32),
        pltpu.VMEM((inner, half), F32),
        pltpu.VMEM((8, 16, 128), F32),
        pltpu.VMEM((16, 16, 128), F32),
        sem((PARTS, 2)),
        sem((PARTS, 2)),
        sem((3,)),
        sem((4,)),
        sem((PARTS, n)),
        sem((PARTS, n)),
        sem((PARTS,)),
        sem((PARTS,)),
        sem((PARTS,)),
        sem((6,)),
        sem((2,)),
        sem((8,)),
        sem((8,)),
        sem((16,)),
        sem((16,)),
    ]
    state = jax.ShapeDtypeStruct(first_moment.shape, F32)
    return pl.pallas_call(
        functools.partial(kernel, multiplier),
        out_shape=(jax.ShapeDtypeStruct(context.shape, BF16), state, state, state),
        in_specs=[pl.BlockSpec(memory_space=pl.ANY)] * 5,
        out_specs=[pl.BlockSpec(memory_space=pl.ANY)] * 4,
        scratch_shapes=scratch,
        compiler_params=pltpu.CompilerParams(
            collective_id=0, has_side_effects=True, vmem_limit_bytes=63 * 2**20
        ),
        cost_estimate=pl.CostEstimate(
            flops=4 * tokens * inner * model, bytes_accessed=40 * 2**20, transcendentals=0
        ),
        name="step",
    )(cotangent, context, weight, first_moment, second_moment)


def solution(mesh):
    in_specs = (
        P("dp", "tensor"),
        P(("dp", "tensor"), None),
        P(None, "tensor"),
        P("dp", "tensor"),
        P("dp", "tensor"),
    )
    out_specs = (P("dp", "tensor"), P("dp", "tensor"), P("dp", "tensor"), P("dp", "tensor"))
    return jax.shard_map(shards, mesh=mesh, in_specs=in_specs, out_specs=out_specs, check_vma=False)
```

time: 465 us -> 136 us (0.29)
  waiting for transfers between devices: 344 us -> 0 us
  Pallas kernels: 0 us -> 128 us
  blocking collectives: 65.7 us -> 0 us
  matrix products: 33.9 us -> 0 us
  between operations: 15.3 us -> 0.65 us
  local copies, waits for them, and re-layouts: 0.01 us -> 7.15 us
  other arithmetic: 6.1 us -> 0 us
    all_gather x1 -> x0, waiting for transfers between devices: 252 us -> none  [shards(): gathered = lax.all_gather(cotangent, 'tensor', axis=0, tiled=True)]
    pallas_call x0 -> x1, Pallas kernels: none -> 128 us  [shards(): pl.pallas_call(functools.partial(kernel, multiplier), out_shape=(jax.Shap...]
    reduce_scatter x1 -> x0, waiting for transfers between devices: 91 us -> none  [shards(): lax.psum_scatter((product * multiplier).astype(jnp.bfloat16), 'dp', scatt...]
    psum x1 -> x0, blocking collectives: 65.7 us -> none  [shards(): lax.psum((weight_local, update_local), ('dp', 'tensor'))]
    dot_general x2 -> x0, matrix products: 33.9 us -> none  [the longest x1 17.4 us: shards(): lax.dot_general(gathered, context, (((0,), (0,)), ((), ())), preferred_el...]
    unnamed x2 -> x10, local copies, waits for them, and re-layouts: 0.01 us -> 7.15 us
    reduce_sum x1 -> x0, other arithmetic: 5.01 us -> none  [shards(): update_local = jnp.sum(update * update)]
  transfers between devices with their start and end apart: 2 -> 0, of which waited for: 2 -> 0; matrix products, arithmetic and copies ran while one was open for 4% -> 0% of each run, Pallas kernels for 0% -> 0%
where the time goes in v1:
time: 136 us
  Pallas kernels  128 us (94%)
  local copies, waits for them, and re-layouts  7.15 us (5%)
    pallas_call x1, Pallas kernels, shards(): pl.pallas_call(functools.partial(kernel, multiplier), out_shape=(jax.Shap...  128 us
    unnamed x10, local copies, waits for them, and re-layouts  7.15 us

profile of v1, /device:TPU:1, one launch (start us, length us, event | category | flops | bytes accessed | tf_op | source)
XLA Modules:
  0.0 135.8 jit_solution(13481984755552370927)
XLA Ops:
  0.6 128.0 %step.1 = (bf16[1024,768]{1,0:T(8,128)(2,1)}, f32[384,768]{1,0:T(8,128)}, f32[384,768]{1,0:T(8,128)}, f32[384,768]{1,0:T(8,128)}) custom-call(bf16[128,6144]{1,0:T(8,128)(2,1)} %cot.1, bf16[1024,768]{1,0:T(8,128)(2,1)} %ctx.1, bf16[6144,768]{1,0:T(8,128)(2,1)} %weight.1, f32[384,768]{1,0:T(8,128)} %first.1, f32[384,768]{1,0:T(8,128)} %second.1), custom_call_target="tpu_custom_call" | custom-call | flops 19327352832 | bytes 41943040 | tf_op jit(solution)/shard_map/step/pallas_call | solution.py:383
  128.6 0.0 copy-start.2
  128.6 2.7 %copy.13 = bf16[1024,768]{1,0:T(8,128)(2,1)} copy(bf16[1024,768]{1,0:T(8,128)(2,1)} %get-tuple-element.8) | data formatting | bytes 3145728
  131.4 0.0 copy-done.2
  131.4 0.0 copy-start.1
  131.4 1.0 copy.14
  132.4 0.7 copy-done.1
  133.1 0.0 copy-start
  133.1 1.0 copy.15
  134.1 0.7 copy-done
  134.8 1.0 copy.16
Async XLA Ops:
  128.6 2.8 %copy-start.2 = (f32[384,768]{1,0:T(8,128)S(1)}, f32[384,768]{1,0:T(8,128)}, u32[]{:S(2)}) copy-start(f32[384,768]{1,0:T(8,128)} %get-tuple-element.9) | copy-start | bytes 3538948
  131.4 1.7 %copy-start.1 = (f32[384,768]{1,0:T(8,128)S(1)}, f32[384,768]{1,0:T(8,128)}, u32[]{:S(2)}) copy-start(f32[384,768]{1,0:T(8,128)} %get-tuple-element.10) | copy-start | bytes 3538948
  133.1 1.7 %copy-start = (f32[384,768]{1,0:T(8,128)S(1)}, f32[384,768]{1,0:T(8,128)}, u32[]{:S(2)}) copy-start(f32[384,768]{1,0:T(8,128)} %get-tuple-element.11) | copy-start | bytes 3538948

commit v2 on v1

v2 whole, which is shorter than its diff:
```python
import functools
import math

import jax
import jax.numpy as jnp
from jax import lax
from jax.experimental import pallas as pl
from jax.experimental.pallas import tpu as pltpu
from jax.sharding import PartitionSpec as P

HEADS = 48
HD = 128
MESH = pl.DeviceIdType.MESH
PARTS = 8
F32 = jnp.float32
BF16 = jnp.bfloat16

MESSAGES = (
    ("z+", 0, 0, 0, 128),
    ("z-", 0, 0, 0, 128),
    ("y", 0, 0, 0, 128),
    ("z+", 0, 1, 0, 80),
    ("z-", 0, 1, 0, 80),
    ("z+", 3, 0, 0, 64),
    ("z-", 1, 0, 64, 128),
    ("y", 3, 0, 80, 128),
    ("y", 1, 0, 80, 128),
    ("z+", 3, 1, 0, 48),
    ("z-", 1, 1, 48, 80),
    ("y", 2, 0, 80, 128),
    ("z+", 3, 1, 0, 32),
    ("z-", 1, 1, 32, 80),
)
SLOTS = 12


def kernel(
    multiplier,
    cot, ctx, weight, first, second,
    cg, mo, va, up, sums,
    gath, wv, cx, cxt, prod, cr, xr, ys, yr, acc, base, one, two,
    own_sem, w_sem, in_sem, gs, gr, gs7, gr7, ds_, dr, xs_, xr_, ysem, s1, r1, s2, r2,
):
    d, t = lax.axis_index("dp"), lax.axis_index("tensor")
    x, yh, c = d // 4, (d // 2) % 2, d % 2
    z, yl = t // 2, t % 2
    half = gath.shape[2] // 2
    rows = cot.shape[0]
    last = PARTS - 1

    def device(x, yh, c, z, yl):
        return ((x * 2 + yh) * 2 + c, z * 2 + yl)

    links = {
        "z+": device(x, yh, c, (z + 1) % 4, yl),
        "z-": device(x, yh, c, (z + 3) % 4, yl),
        "y": device(x, yh, c, z, 1 - yl),
    }
    sibling = device(x, yh, 1 - c, z, yl)

    def offset(s, h):
        r = s % 4
        return ((2 + 3 * r + 3 * (r * (r - 1) // 2)) * (1 + 2 * h)) % 4

    def owner(s, h):
        oy = (yh + 1 - s // 4) % 2
        h = (h + (1 - c) * (s // last)) % 2
        return (((x + offset(s, h)) % 4) * 2 + oy) * 2 + h

    def own_copy(s, h):
        at = pl.multiple_of(owner(s, h) * half, 128)
        return pltpu.make_async_copy(
            cot.at[:, pl.ds(at, half)],
            gath.at[s, pl.ds(pl.multiple_of(t * rows, rows), rows), pl.ds(h * half, half)],
            own_sem.at[s, h],
        )

    def w_copy(s, h):
        at = pl.multiple_of(owner(s, h) * half, 128)
        return pltpu.make_async_copy(
            weight.at[pl.ds(at, half)], wv.at[s, pl.ds(h * half, half)], w_sem.at[s, h]
        )

    ctx_copy = pltpu.make_async_copy(ctx, cx, in_sem.at[0])
    first_copy = pltpu.make_async_copy(first, mo, in_sem.at[1])
    second_copy = pltpu.make_async_copy(second, va, in_sem.at[2])

    def message(s, k, received, part=None):
        link, dz, yb, lo, hi = MESSAGES[k]
        if received:
            dz = (dz + {"z+": 3, "z-": 1, "y": 0}[link]) % 4
            yb = 1 - yb if link == "y" else yb
        block = ((z + dz) % 4) * 2 + (1 - yl if yb else yl)
        at = pl.ds(pl.multiple_of(block * rows + lo, 16), hi - lo)
        slot = k if k < SLOTS else k - SLOTS + 9
        if part is None:
            ref, sent, got = gath.at[s, at], gs.at[s, slot], gr.at[s, slot]
        else:
            ref = gath.at[s, at, pl.ds(part * half, half)]
            sent, got = gs7.at[part, slot], gr7.at[part, slot]
        return pltpu.make_async_remote_copy(
            src_ref=ref, dst_ref=ref, send_sem=sent, recv_sem=got,
            device_id=links[link], device_id_type=MESH,
        )

    def send(s, *ks, part=None):
        for k in ks:
            message(s, k, False, part).start()

    def arrive(s, *ks, part=None):
        for k in ks:
            message(s, k, True, part).wait_recv()

    def by_parity(s, action):
        @pl.when(s % 2 == 0)
        def _():
            for k in (9, 10):
                action(k)

        @pl.when(s % 2 == 1)
        def _():
            for k in (12, 13):
                action(k)

    def stage_a(s):
        for h in range(2):
            own_copy(s, h).wait()
        send(s, 0, 1, 2)

    def stage_b(s):
        arrive(s, 2)
        send(s, 3, 4)
        arrive(s, 0)
        send(s, 5, 7)
        arrive(s, 1)
        send(s, 6, 8)

    def stage_c(s):
        arrive(s, 3)
        arrive(s, 4)
        by_parity(s, lambda k: send(s, k))
        arrive(s, 6)
        send(s, 11)

    def core_copy(s, part=None):
        src = prod.at[s, 1 - c] if part is None else prod.at[s, part]
        return pltpu.make_async_remote_copy(
            src_ref=src, dst_ref=cr.at[s], send_sem=ds_.at[s], recv_sem=dr.at[s],
            device_id=sibling, device_id_type=MESH,
        )

    def x_copy(s):
        dx = offset(s, c)
        slot = (1 - s // 4) * 3 + (dx + 3) % 4
        return pltpu.make_async_remote_copy(
            src_ref=prod.at[s, c], dst_ref=xr.at[slot], send_sem=xs_.at[s], recv_sem=xr_.at[slot],
            device_id=device((x + dx) % 4, yh, c, z, yl), device_id_type=MESH,
        )

    def x_arrive(slot):
        pltpu.make_async_remote_copy(
            src_ref=xr.at[slot], dst_ref=xr.at[slot], send_sem=xs_.at[0], recv_sem=xr_.at[slot],
            device_id=sibling, device_id_type=MESH,
        ).wait_recv()

    y_copy = pltpu.make_async_remote_copy(
        src_ref=ys, dst_ref=yr, send_sem=ysem.at[0], recv_sem=ysem.at[1],
        device_id=device(x, 1 - yh, c, z, yl), device_id_type=MESH,
    )

    group1 = [
        ((x + dx) % 4, (c + dc) % 2, (dx * 2 + dc)) for dx in range(4) for dc in range(2) if dx or dc
    ]
    y = yh * 2 + yl
    group2 = [
        ((y + dy) % 4, (z + dz) % 4, (dy * 4 + dz)) for dy in range(4) for dz in range(4) if dy or dz
    ]

    def one_copy(px, pc, slot):
        return pltpu.make_async_remote_copy(
            src_ref=one.at[0], dst_ref=one.at[slot], send_sem=s1.at[slot], recv_sem=r1.at[slot],
            device_id=device(px, yh, pc, z, yl), device_id_type=MESH,
        )

    def two_copy(py, pz, slot):
        return pltpu.make_async_remote_copy(
            src_ref=two.at[0], dst_ref=two.at[slot], send_sem=s2.at[slot], recv_sem=r2.at[slot],
            device_id=device(x, py // 2, c, pz, py % 2), device_id_type=MESH,
        )

    for s in range(PARTS):
        for h in range(2):
            own_copy(s, h).start()
        if s == 0:
            ctx_copy.start()
    for s in range(PARTS):
        for h in range(2):
            w_copy(s, h).start()
    first_copy.start()
    second_copy.start()

    barrier = pltpu.get_barrier_semaphore()
    for px, pc, _ in group1:
        pl.semaphore_signal(barrier, inc=1, device_id=device(px, yh, pc, z, yl), device_id_type=MESH)
    for py, pz, _ in group2:
        pl.semaphore_signal(barrier, inc=1, device_id=device(x, py // 2, c, pz, py % 2), device_id_type=MESH)
    pl.semaphore_wait(barrier, len(group1) + len(group2))

    stage_a(0)
    ctx_copy.wait()
    for k in range(cx.shape[0] // 128):
        cxt[:, k * 128 : (k + 1) * 128] = cx[k * 128 : (k + 1) * 128, :].T

    def product(s, lo, hi):
        for start in range(lo, hi, 256):
            width = min(256, hi - start)
            value = jnp.dot(cxt[...], gath[s, :, start : start + width], preferred_element_type=F32)
            value = (value * multiplier).astype(BF16)
            for k in range(0, width, 128):
                column = start + k
                prod[s, column // half, :, column % half : column % half + 128] = value[:, k : k + 128]

    def context_part(s, final):
        if not final:
            for h in range(2):
                w_copy(s, h).wait()

        @pl.loop(0, acc.shape[1] // 256)
        def _(n):
            cols = pl.ds(pl.multiple_of(n * 256, 256), 256)
            value = jnp.dot(gath[s], wv[s, :, cols], preferred_element_type=F32)
            if final:
                cg[:, cols] = ((acc[:, cols] + value) * multiplier).astype(BF16)
            else:
                acc[:, cols] += value

    def whole(s):
        arrive(s, 5, 7, 8)
        by_parity(s, lambda k: arrive(s, k))
        arrive(s, 11)
        product(s, 0, 2 * half)
        core_copy(s).start()

    def cores_sum(s):
        core_copy(s).wait_recv()

        @pl.when(s % 4 != 3)
        def _():
            prod[s, c] = (prod[s, c].astype(F32) + cr[s].astype(F32)).astype(BF16)
            x_copy(s).start()

    acc[...] = jnp.zeros_like(acc)

    @pl.loop(0, last)
    def _(i):
        stage_a(i + 1)
        stage_b(i)

        @pl.when(i > 0)
        def _():
            stage_c(i - 1)

        @pl.when(i > 1)
        def _():
            s = i - 2
            whole(s)
            context_part(s, False)
            cores_sum(s)

            @pl.when(s == 4)
            def _():
                total = prod[3, c].astype(F32) + cr[3].astype(F32)
                for slot in range(3, 6):
                    x_arrive(slot)
                    total += xr[slot].astype(F32)
                ys[...] = total.astype(BF16)
                y_copy.start()

    arrive(last, 2, 0, 1)
    send(last, 3, 4, 5, 7, 6, 8, part=0)
    send(last, 3, 4, 5, 7, 6, 8, part=1)
    stage_c(last - 1)
    whole(last - 2)
    context_part(last - 2, False)
    cores_sum(last - 2)
    arrive(last, 3, 4, part=0)
    send(last, 12, 13, part=0)
    arrive(last, 6, part=0)
    send(last, 11, part=0)
    whole(last - 1)
    arrive(last, 3, 4, part=1)
    send(last, 12, 13, part=1)
    arrive(last, 6, part=1)
    send(last, 11, part=1)
    cores_sum(last - 1)
    arrive(last, 5, 7, 8, 12, 13, 11, part=0)
    product(last, 0, half)
    core_copy(last, 0).start()
    y_copy.wait_recv()
    for slot in range(3):
        x_arrive(slot)
    core_copy(last, 0).wait_recv()
    for k in range(half // 128):
        cols = slice(k * 128, (k + 1) * 128)
        total = yr[:, cols].astype(F32) + cr[last, :, cols].astype(F32)
        for slot in range(3):
            total += xr[slot, :, cols].astype(F32)
        base[cols, :] = total.T
    first_copy.wait()
    second_copy.wait()
    for h in range(2):
        w_copy(last, h).wait()
    arrive(last, 5, 7, 8, 12, 13, 11, part=1)

    def fold(value):
        total = value[0:8, 0:128]
        for r in range(value.shape[0] // 8):
            for k in range(value.shape[1] // 128):
                if r or k:
                    total += value[r * 8 : (r + 1) * 8, k * 128 : (k + 1) * 128]
        return total[0:4] + total[4:8]

    u_sum, w_sum = jnp.zeros((4, 128), F32), jnp.zeros((4, 128), F32)
    for k in range(half // 128):
        cols = slice(k * 128, (k + 1) * 128)
        at = slice(half + k * 128, half + (k + 1) * 128)
        mine = jnp.dot(cxt[...], gath[last, :, at], preferred_element_type=F32) * multiplier
        g = base[cols, :] + mine.T
        w = wv[last, at, :].astype(F32)
        m = 0.9 * mo[cols, :] + 0.1 * g
        v = 0.95 * va[cols, :] + 0.05 * g * g
        u = m / (jnp.sqrt(v) + 1e-06) + 0.1 * w
        mo[cols, :] = m
        va[cols, :] = v
        up[cols, :] = u
        u_sum += fold(u * u)
        w_sum += fold(w * w)
    one[0, 0:4] = u_sum
    one[0, 4:8] = w_sum
    for px, pc, slot in group1:
        one_copy(px, pc, slot).start()
    context_part(last - 1, False)
    for px, pc, slot in group1:
        one_copy(px, pc, slot).wait_recv()
    total = one[0]
    for _, _, slot in group1:
        total += one[slot]
    two[0] = total
    for py, pz, slot in group2:
        two_copy(py, pz, slot).start()
    context_part(last, True)

    @pl.loop(0, PARTS)
    def _(s):
        for k in range(3):
            message(s, k, False).wait_send()

        @pl.when(s < last)
        def _():
            for k in (3, 4, 5, 6, 7, 8, 11):
                message(s, k, False).wait_send()
            by_parity(s, lambda k: message(s, k, False).wait_send())
            core_copy(s).wait_send()

        @pl.when(s % 4 != 3)
        def _():
            x_copy(s).wait_send()

    for part in range(2):
        for k in (3, 4, 5, 6, 7, 8, 11, 12, 13):
            message(last, k, False, part).wait_send()
    core_copy(last, 0).wait_send()
    y_copy.wait_send()
    for px, pc, slot in group1:
        one_copy(px, pc, slot).wait_send()
    for py, pz, slot in group2:
        two_copy(py, pz, slot).wait_recv()
    total = two[0]
    for _, _, slot in group2:
        total += two[slot]
    sums[...] = total
    for py, pz, slot in group2:
        two_copy(py, pz, slot).wait_send()


def finish(cg, mo, va, up, sums, cg_out, mo_out, va_out, la_out, la, sem):
    copies = [
        pltpu.make_async_copy(src, dst, sem.at[k])
        for k, (src, dst) in enumerate(((cg, cg_out), (mo, mo_out), (va, va_out)))
    ]
    for copy in copies:
        copy.start()
    u_total = jnp.sum(sums[0:4, :], keepdims=True)
    w_total = jnp.sum(sums[4:8, :], keepdims=True)
    la[...] = up[...] * (jnp.sqrt(w_total) / jnp.sqrt(u_total + 1e-06))
    copies.append(pltpu.make_async_copy(la, la_out, sem.at[3]))
    copies[-1].start()
    for copy in copies:
        copy.wait()


def shards(context, cotangent, weight, first_moment, second_moment):
    multiplier = 1.0 / math.sqrt(HEADS * HD)
    tokens, inner = context.shape
    rows, model = cotangent.shape
    part = model // PARTS
    half = part // 2
    sem = pltpu.SemaphoreType.DMA
    n = SLOTS
    scratch = [
        pltpu.VMEM((PARTS, tokens, part), BF16),
        pltpu.VMEM((PARTS, part, inner), BF16),
        pltpu.VMEM((tokens, inner), BF16),
        pltpu.VMEM((inner, tokens), BF16),
        pltpu.VMEM((PARTS, 2, inner, half), BF16),
        pltpu.VMEM((PARTS, inner, half), BF16),
        pltpu.VMEM((6, inner, half), BF16),
        pltpu.VMEM((inner, half), BF16),
        pltpu.VMEM((inner, half), BF16),
        pltpu.VMEM((tokens, inner), F32),
        pltpu.VMEM((half, inner), F32),
        pltpu.VMEM((8, 8, 128), F32),
        pltpu.VMEM((16, 8, 128), F32),
        sem((PARTS, 2)),
        sem((PARTS, 2)),
        sem((3,)),
        sem((PARTS, n)),
        sem((PARTS, n)),
        sem((2, n)),
        sem((2, n)),
        sem((PARTS,)),
        sem((PARTS,)),
        sem((PARTS,)),
        sem((6,)),
        sem((2,)),
        sem((8,)),
        sem((8,)),
        sem((16,)),
        sem((16,)),
    ]
    vmem = pl.BlockSpec(memory_space=pltpu.VMEM)
    anywhere = pl.BlockSpec(memory_space=pl.ANY)
    state = pltpu.VMEM(first_moment.shape, F32)
    results = pl.pallas_call(
        functools.partial(kernel, multiplier),
        out_shape=(pltpu.VMEM(context.shape, BF16), state, state, state, pltpu.VMEM((8, 128), F32)),
        in_specs=[anywhere] * 5,
        out_specs=[vmem] * 5,
        scratch_shapes=scratch,
        compiler_params=pltpu.CompilerParams(
            collective_id=0, has_side_effects=True, vmem_limit_bytes=56 * 2**20
        ),
        cost_estimate=pl.CostEstimate(
            flops=4 * tokens * inner * model, bytes_accessed=40 * 2**20, transcendentals=0
        ),
        name="step",
    )(cotangent, context, weight, first_moment, second_moment)
    results = [pltpu.with_memory_space_constraint(r, pltpu.VMEM) for r in results]
    state = jax.ShapeDtypeStruct(first_moment.shape, F32)
    return pl.pallas_call(
        finish,
        out_shape=(jax.ShapeDtypeStruct(context.shape, BF16), state, state, state),
        in_specs=[vmem] * 5,
        out_specs=[anywhere] * 4,
        scratch_shapes=[pltpu.VMEM(first_moment.shape, F32), sem((4,))],
        compiler_params=pltpu.CompilerParams(vmem_limit_bytes=4 * 2**20),
        name="finish",
    )(*results)


def solution(mesh):
    in_specs = (
        P("dp", "tensor"),
        P(("dp", "tensor"), None),
        P(None, "tensor"),
        P("dp", "tensor"),
        P("dp", "tensor"),
    )
    out_specs = (P("dp", "tensor"), P("dp", "tensor"), P("dp", "tensor"), P("dp", "tensor"))
    return jax.shard_map(shards, mesh=mesh, in_specs=in_specs, out_specs=out_specs, check_vma=False)
```

time: 136 us -> 129 us (0.949)
  local copies, waits for them, and re-layouts: 7.15 us -> 0 us
    unnamed x10 -> x0, local copies, waits for them, and re-layouts: 7.15 us -> none
    pallas_call x1 -> x2, Pallas kernels: 128 us -> 128 us  [the longest x1 126 us: shards(): pl.pallas_call(functools.partial(kernel, multiplier), out_shape=(pltpu.VM...]
where the time goes in v2:
time: 129 us
  Pallas kernels  128 us (99%)
    pallas_call x1, Pallas kernels, shards(): pl.pallas_call(functools.partial(kernel, multiplier), out_shape=(pltpu.VM...  126 us

profile of v2, /device:TPU:1, one launch (start us, length us, event | category | flops | bytes accessed | tf_op | source)
XLA Modules:
  0.0 128.7 jit_solution(2989328378190994253)
XLA Ops:
  0.6 125.7 %step.1 = (bf16[1024,768]{1,0:T(8,128)(2,1)S(1)}, f32[384,768]{1,0:T(8,128)S(1)}, f32[384,768]{1,0:T(8,128)S(1)}, f32[384,768]{1,0:T(8,128)S(1)}, f32[8,128]{1,0:T(8,128)S(1)}) custom-call(bf16[128,6144]{1,0:T(8,128)(2,1)} %cot.1, bf16[1024,768]{1,0:T(8,128)(2,1)} %ctx.1, bf16[6144,768]{1,0:T(8,128)(2,1)} %weight.1, f32[384,768]{1,0:T(8,128)} %first.1, ...), custom_call_target="tpu_custom_call" | custom-call | flops 19327352832 | bytes 41943040 | tf_op jit(solution)/shard_map/step/pallas_call | solution.py:444
  126.3 2.3 %finish.1 = (bf16[1024,768]{1,0:T(8,128)(2,1)}, f32[384,768]{1,0:T(8,128)}, f32[384,768]{1,0:T(8,128)}, f32[384,768]{1,0:T(8,128)}) custom-call(bf16[1024,768]{1,0:T(8,128)(2,1)S(1)} %get-tuple-element.9.cg, f32[384,768]{1,0:T(8,128)S(1)} %get-tuple-element.10.mo, f32[384,768]{1,0:T(8,128)S(1)} %get-tuple-element.11.va, ...), custom_call_target="tpu_custom_call" | custom-call | tf_op jit(solution)/shard_map/finish/pallas_call | solution.py:460

commit v3 on v2

--- a/solution.py
+++ b/solution.py
@@ -16,22 +16,27 @@
 BF16 = jnp.bfloat16
 
 MESSAGES = (
-    ("z+", 0, 0, 0, 128),
-    ("z-", 0, 0, 0, 128),
-    ("y", 0, 0, 0, 128),
-    ("z+", 0, 1, 0, 80),
-    ("z-", 0, 1, 0, 80),
-    ("z+", 3, 0, 0, 64),
-    ("z-", 1, 0, 64, 128),
-    ("y", 3, 0, 80, 128),
-    ("y", 1, 0, 80, 128),
-    ("z+", 3, 1, 0, 48),
-    ("z-", 1, 1, 48, 80),
-    ("y", 2, 0, 80, 128),
-    ("z+", 3, 1, 0, 32),
-    ("z-", 1, 1, 32, 80),
+    ("z+", 0, 0),
+    ("z-", 0, 0),
+    ("y", 0, 0),
+    ("z+", 0, 1),
+    ("z-", 0, 1),
+    ("z+", 3, 0),
+    ("z-", 1, 0),
+    ("y", 3, 0),
+    ("y", 1, 0),
+    ("z+", 3, 1),
+    ("z-", 1, 1),
+    ("y", 2, 0),
 )
-SLOTS = 12
+PLAN = ((64, 32), (64, 32), (64, 32), (64, 32), (96, 48), (112, 64), (112, 48), (80, 32))
+
+
+def span(k, plan):
+    first, plus = plan
+    return ((0, 128), (0, first), (0, 64), (64, 128), (first, 128), (0, plus), (plus, first))[
+        (0, 0, 0, 1, 1, 2, 3, 4, 4, 5, 6, 4)[k]
+    ]
 
 
 def kernel(
@@ -85,62 +90,78 @@
     first_copy = pltpu.make_async_copy(first, mo, in_sem.at[1])
     second_copy = pltpu.make_async_copy(second, va, in_sem.at[2])
 
-    def message(s, k, received, part=None):
-        link, dz, yb, lo, hi = MESSAGES[k]
+    def message(s, k, received, plan, part=None):
+        link, dz, yb = MESSAGES[k]
+        lo, hi = span(k, plan)
         if received:
             dz = (dz + {"z+": 3, "z-": 1, "y": 0}[link]) % 4
             yb = 1 - yb if link == "y" else yb
         block = ((z + dz) % 4) * 2 + (1 - yl if yb else yl)
         at = pl.ds(pl.multiple_of(block * rows + lo, 16), hi - lo)
-        slot = k if k < SLOTS else k - SLOTS + 9
         if part is None:
-            ref, sent, got = gath.at[s, at], gs.at[s, slot], gr.at[s, slot]
+            ref, sent, got = gath.at[s, at], gs.at[s, k], gr.at[s, k]
         else:
             ref = gath.at[s, at, pl.ds(part * half, half)]
-            sent, got = gs7.at[part, slot], gr7.at[part, slot]
+            sent, got = gs7.at[part, k], gr7.at[part, k]
         return pltpu.make_async_remote_copy(
             src_ref=ref, dst_ref=ref, send_sem=sent, recv_sem=got,
             device_id=links[link], device_id_type=MESH,
         )
 
-    def send(s, *ks, part=None):
+    def by_plan(s, action):
+        if isinstance(s, int):
+            action(PLAN[s])
+            return
+        lo = 0
+        for hi in range(1, last + 1):
+            if hi == last or PLAN[hi] != PLAN[lo]:
+
+                @pl.when((s >= lo) & (s < hi))
+                def _(plan=PLAN[lo]):
+                    action(plan)
+
+                lo = hi
+
+    def send(s, plan, *ks, part=None):
         for k in ks:
-            message(s, k, False, part).start()
-
-    def arrive(s, *ks, part=None):
+            message(s, k, False, plan, part).start()
+
+    def arrive(s, plan, *ks, part=None):
         for k in ks:
-            message(s, k, True, part).wait_recv()
-
-    def by_parity(s, action):
-        @pl.when(s % 2 == 0)
-        def _():
-            for k in (9, 10):
-                action(k)
-
-        @pl.when(s % 2 == 1)
-        def _():
-            for k in (12, 13):
-                action(k)
+            message(s, k, True, plan, part).wait_recv()
 
     def stage_a(s):
         for h in range(2):
             own_copy(s, h).wait()
-        send(s, 0, 1, 2)
-
-    def stage_b(s):
-        arrive(s, 2)
-        send(s, 3, 4)
-        arrive(s, 0)
-        send(s, 5, 7)
-        arrive(s, 1)
-        send(s, 6, 8)
-
-    def stage_c(s):
-        arrive(s, 3)
-        arrive(s, 4)
-        by_parity(s, lambda k: send(s, k))
-        arrive(s, 6)
-        send(s, 11)
+        send(s, PLAN[0], 0, 1, 2)
+
+    def stage_b(s, part=None, first=True):
+        def steps(plan):
+            if first:
+                arrive(s, plan, 2)
+            send(s, plan, 3, 4, part=part)
+            if first:
+                arrive(s, plan, 0)
+            send(s, plan, 5, 7, part=part)
+            if first:
+                arrive(s, plan, 1)
+            send(s, plan, 6, 8, part=part)
+
+        by_plan(s, steps)
+
+    def stage_c(s, part=None):
+        def steps(plan):
+            arrive(s, plan, 3, part=part)
+            send(s, plan, 9, part=part)
+            arrive(s, plan, 4, part=part)
+            send(s, plan, 10, part=part)
+            arrive(s, plan, 6, part=part)
+            send(s, plan, 11, part=part)
+
+        by_plan(s, steps)
+
+    def gathered(s, part=None):
+        by_plan(s, lambda plan: arrive(s, plan, 5, 7, 8, 9, 10, 11, part=part))
 
     def core_copy(s, part=None):
         src = prod.at[s, 1 - c] if part is None else prod.at[s, part]
@@ -235,9 +256,7 @@
                 acc[:, cols] += value
 
     def whole(s):
-        arrive(s, 5, 7, 8)
-        by_parity(s, lambda k: arrive(s, k))
-        arrive(s, 11)
+        gathered(s)
         product(s, 0, 2 * half)
         core_copy(s).start()
 
@@ -253,12 +272,19 @@
 
     @pl.loop(0, last)
     def _(i):
-        stage_a(i + 1)
+        @pl.when(i < last - 1)
+        def _():
+            stage_a(i + 1)
+
         stage_b(i)
 
         @pl.when(i > 0)
         def _():
             stage_c(i - 1)
+
+        @pl.when(i == last - 1)
+        def _():
+            stage_a(last)
 
         @pl.when(i > 1)
         def _():
@@ -267,7 +293,7 @@
             context_part(s, False)
             cores_sum(s)
 
-            @pl.when(s == 4)
+            @pl.when(s == 3)
             def _():
                 total = prod[3, c].astype(F32) + cr[3].astype(F32)
                 for slot in range(3, 6):
@@ -276,24 +302,17 @@
                 ys[...] = total.astype(BF16)
                 y_copy.start()
 
-    arrive(last, 2, 0, 1)
-    send(last, 3, 4, 5, 7, 6, 8, part=0)
-    send(last, 3, 4, 5, 7, 6, 8, part=1)
     stage_c(last - 1)
+    stage_b(last, part=0)
+    stage_b(last, part=1, first=False)
     whole(last - 2)
+    cores_sum(last - 2)
+    whole(last - 1)
+    cores_sum(last - 1)
+    stage_c(last, part=0)
+    stage_c(last, part=1)
     context_part(last - 2, False)
-    cores_sum(last - 2)
-    arrive(last, 3, 4, part=0)
-    send(last, 12, 13, part=0)
-    arrive(last, 6, part=0)
-    send(last, 11, part=0)
-    whole(last - 1)
-    arrive(last, 3, 4, part=1)
-    send(last, 12, 13, part=1)
-    arrive(last, 6, part=1)
-    send(last, 11, part=1)
-    cores_sum(last - 1)
-    arrive(last, 5, 7, 8, 12, 13, 11, part=0)
+    gathered(last, part=0)
     product(last, 0, half)
     core_copy(last, 0).start()
     y_copy.wait_recv()
@@ -310,7 +329,7 @@
     second_copy.wait()
     for h in range(2):
         w_copy(last, h).wait()
-    arrive(last, 5, 7, 8, 12, 13, 11, part=1)
+    gathered(last, part=1)
 
     def fold(value):
         total = value[0:8, 0:128]
@@ -353,13 +372,15 @@
     @pl.loop(0, PARTS)
     def _(s):
         for k in range(3):
-            message(s, k, False).wait_send()
+            message(s, k, False, PLAN[0]).wait_send()
 
         @pl.when(s < last)
         def _():
-            for k in (3, 4, 5, 6, 7, 8, 11):
-                message(s, k, False).wait_send()
-            by_parity(s, lambda k: message(s, k, False).wait_send())
+            def steps(plan):
+                for k in range(3, len(MESSAGES)):
+                    message(s, k, False, plan).wait_send()
+
+            by_plan(s, steps)
             core_copy(s).wait_send()
 
         @pl.when(s % 4 != 3)
@@ -367,8 +388,8 @@
             x_copy(s).wait_send()
 
     for part in range(2):
-        for k in (3, 4, 5, 6, 7, 8, 11, 12, 13):
-            message(last, k, False, part).wait_send()
+        for k in range(3, len(MESSAGES)):
+            message(last, k, False, PLAN[last], part).wait_send()
     core_copy(last, 0).wait_send()
     y_copy.wait_send()
     for px, pc, slot in group1:
@@ -406,7 +427,7 @@
     part = model // PARTS
     half = part // 2
     sem = pltpu.SemaphoreType.DMA
-    n = SLOTS
+    n = len(MESSAGES)
     scratch = [
         pltpu.VMEM((PARTS, tokens, part), BF16),
         pltpu.VMEM((PARTS, part, inner), BF16),

time: 129 us -> 124 us (0.961)
  Pallas kernels: 128 us -> 123 us
    pallas_call x1, Pallas kernels: 126 us -> 121 us  [shards(): pl.pallas_call(functools.partial(kernel, multiplier), out_shape=(pltpu.VM...]
where the time goes in v3:
time: 124 us
  Pallas kernels  123 us (99%)
    pallas_call x1, Pallas kernels, shards(): pl.pallas_call(functools.partial(kernel, multiplier), out_shape=(pltpu.VM...  121 us

profile of v3, /device:TPU:1, one launch (start us, length us, event | category | flops | bytes accessed | tf_op | source)
XLA Modules:
  0.0 123.6 jit_solution(12013224228854987756)
XLA Ops:
  0.6 120.6 %step.1 = (bf16[1024,768]{1,0:T(8,128)(2,1)S(1)}, f32[384,768]{1,0:T(8,128)S(1)}, f32[384,768]{1,0:T(8,128)S(1)}, f32[384,768]{1,0:T(8,128)S(1)}, f32[8,128]{1,0:T(8,128)S(1)}) custom-call(bf16[128,6144]{1,0:T(8,128)(2,1)} %cot.1, bf16[1024,768]{1,0:T(8,128)(2,1)} %ctx.1, bf16[6144,768]{1,0:T(8,128)(2,1)} %weight.1, f32[384,768]{1,0:T(8,128)} %first.1, ...), custom_call_target="tpu_custom_call" | custom-call | flops 19327352832 | bytes 41943040 | tf_op jit(solution)/shard_map/step/pallas_call | solution.py:465
  121.2 2.3 %finish.1 = (bf16[1024,768]{1,0:T(8,128)(2,1)}, f32[384,768]{1,0:T(8,128)}, f32[384,768]{1,0:T(8,128)}, f32[384,768]{1,0:T(8,128)}) custom-call(bf16[1024,768]{1,0:T(8,128)(2,1)S(1)} %get-tuple-element.9.cg, f32[384,768]{1,0:T(8,128)S(1)} %get-tuple-element.10.mo, f32[384,768]{1,0:T(8,128)S(1)} %get-tuple-element.11.va, ...), custom_call_target="tpu_custom_call" | custom-call | tf_op jit(solution)/shard_map/finish/pallas_call | solution.py:481

commit v4 on v3

--- a/solution.py
+++ b/solution.py
@@ -43,7 +43,7 @@
     multiplier,
     cot, ctx, weight, first, second,
     cg, mo, va, up, sums,
-    gath, wv, cx, cxt, prod, cr, xr, ys, yr, acc, base, one, two,
+    gath, wv, cx, cxt, prod, cr, xr, ys, yr, acc, mine, one, two,
     own_sem, w_sem, in_sem, gs, gr, gs7, gr7, ds_, dr, xs_, xr_, ysem, s1, r1, s2, r2,
 ):
     d, t = lax.axis_index("dp"), lax.axis_index("tensor")
@@ -302,19 +302,23 @@
                 ys[...] = total.astype(BF16)
                 y_copy.start()
 
+    whole(last - 2)
     stage_c(last - 1)
+    cores_sum(last - 2)
     stage_b(last, part=0)
     stage_b(last, part=1, first=False)
-    whole(last - 2)
-    cores_sum(last - 2)
     whole(last - 1)
     cores_sum(last - 1)
     stage_c(last, part=0)
     stage_c(last, part=1)
-    context_part(last - 2, False)
     gathered(last, part=0)
     product(last, 0, half)
     core_copy(last, 0).start()
+    gathered(last, part=1)
+    for start, width in ((0, 256), (256, 128)):
+        value = jnp.dot(cxt[...], gath[last, :, half + start : half + start + width], preferred_element_type=F32)
+        mine[:, start : start + width] = value * multiplier
+    context_part(last - 2, False)
     y_copy.wait_recv()
     for slot in range(3):
         x_arrive(slot)
@@ -324,12 +328,11 @@
         total = yr[:, cols].astype(F32) + cr[last, :, cols].astype(F32)
         for slot in range(3):
             total += xr[slot, :, cols].astype(F32)
-        base[cols, :] = total.T
+        mine[:, cols] += total
     first_copy.wait()
     second_copy.wait()
     for h in range(2):
         w_copy(last, h).wait()
-    gathered(last, part=1)
 
     def fold(value):
         total = value[0:8, 0:128]
@@ -343,8 +346,7 @@
     for k in range(half // 128):
         cols = slice(k * 128, (k + 1) * 128)
         at = slice(half + k * 128, half + (k + 1) * 128)
-        mine = jnp.dot(cxt[...], gath[last, :, at], preferred_element_type=F32) * multiplier
-        g = base[cols, :] + mine.T
+        g = mine[:, cols].T
         w = wv[last, at, :].astype(F32)
         m = 0.9 * mo[cols, :] + 0.1 * g
         v = 0.95 * va[cols, :] + 0.05 * g * g
@@ -439,7 +441,7 @@
         pltpu.VMEM((inner, half), BF16),
         pltpu.VMEM((inner, half), BF16),
         pltpu.VMEM((tokens, inner), F32),
-        pltpu.VMEM((half, inner), F32),
+        pltpu.VMEM((inner, half), F32),
         pltpu.VMEM((8, 8, 128), F32),
         pltpu.VMEM((16, 8, 128), F32),
         sem((PARTS, 2)),

time: 124 us -> 121 us (0.976)
  Pallas kernels: 123 us -> 120 us
    pallas_call x1, Pallas kernels: 121 us -> 118 us  [shards(): pl.pallas_call(functools.partial(kernel, multiplier), out_shape=(pltpu.VM...]
where the time goes in v4:
time: 121 us
  Pallas kernels  120 us (99%)
    pallas_call x1, Pallas kernels, shards(): pl.pallas_call(functools.partial(kernel, multiplier), out_shape=(pltpu.VM...  118 us

profile of v4, /device:TPU:1, one launch (start us, length us, event | category | flops | bytes accessed | tf_op | source)
XLA Modules:
  0.0 120.8 jit_solution(16172219354631734831)
XLA Ops:
  0.6 117.8 %step.1 = (bf16[1024,768]{1,0:T(8,128)(2,1)S(1)}, f32[384,768]{1,0:T(8,128)S(1)}, f32[384,768]{1,0:T(8,128)S(1)}, f32[384,768]{1,0:T(8,128)S(1)}, f32[8,128]{1,0:T(8,128)S(1)}) custom-call(bf16[128,6144]{1,0:T(8,128)(2,1)} %cot.1, bf16[1024,768]{1,0:T(8,128)(2,1)} %ctx.1, bf16[6144,768]{1,0:T(8,128)(2,1)} %weight.1, f32[384,768]{1,0:T(8,128)} %first.1, ...), custom_call_target="tpu_custom_call" | custom-call | flops 19327352832 | bytes 41943040 | tf_op jit(solution)/shard_map/step/pallas_call | solution.py:467
  118.4 2.3 %finish.1 = (bf16[1024,768]{1,0:T(8,128)(2,1)}, f32[384,768]{1,0:T(8,128)}, f32[384,768]{1,0:T(8,128)}, f32[384,768]{1,0:T(8,128)}) custom-call(bf16[1024,768]{1,0:T(8,128)(2,1)S(1)} %get-tuple-element.9.cg, f32[384,768]{1,0:T(8,128)S(1)} %get-tuple-element.10.mo, f32[384,768]{1,0:T(8,128)S(1)} %get-tuple-element.11.va, ...), custom_call_target="tpu_custom_call" | custom-call | tf_op jit(solution)/shard_map/finish/pallas_call | solution.py:483

commit v5 on v4

--- a/solution.py
+++ b/solution.py
@@ -319,6 +319,27 @@
         value = jnp.dot(cxt[...], gath[last, :, half + start : half + start + width], preferred_element_type=F32)
         mine[:, start : start + width] = value * multiplier
     context_part(last - 2, False)
+    first_copy.wait()
+    second_copy.wait()
+    for h in range(2):
+        w_copy(last, h).wait()
+
+    def fold(value):
+        total = value[0:8, 0:128]
+        for r in range(value.shape[0] // 8):
+            for k in range(value.shape[1] // 128):
+                if r or k:
+                    total += value[r * 8 : (r + 1) * 8, k * 128 : (k + 1) * 128]
+        return total[0:4] + total[4:8]
+
+    w_sum = jnp.zeros((4, 128), F32)
+    for k in range(half // 128):
+        cols = slice(k * 128, (k + 1) * 128)
+        w = wv[last, half + k * 128 : half + (k + 1) * 128, :].astype(F32)
+        w_sum += fold(w * w)
+        up[cols, :] = 0.1 * w
+        mo[cols, :] = 0.9 * mo[cols, :]
+        va[cols, :] = 0.95 * va[cols, :]
     y_copy.wait_recv()
     for slot in range(3):
         x_arrive(slot)
@@ -329,33 +350,17 @@
         for slot in range(3):
             total += xr[slot, :, cols].astype(F32)
         mine[:, cols] += total
-    first_copy.wait()
-    second_copy.wait()
-    for h in range(2):
-        w_copy(last, h).wait()
-
-    def fold(value):
-        total = value[0:8, 0:128]
-        for r in range(value.shape[0] // 8):
-            for k in range(value.shape[1] // 128):
-                if r or k:
-                    total += value[r * 8 : (r + 1) * 8, k * 128 : (k + 1) * 128]
-        return total[0:4] + total[4:8]
-
-    u_sum, w_sum = jnp.zeros((4, 128), F32), jnp.zeros((4, 128), F32)
+    u_sum = jnp.zeros((4, 128), F32)
     for k in range(half // 128):
         cols = slice(k * 128, (k + 1) * 128)
-        at = slice(half + k * 128, half + (k + 1) * 128)
         g = mine[:, cols].T
-        w = wv[last, at, :].astype(F32)
-        m = 0.9 * mo[cols, :] + 0.1 * g
-        v = 0.95 * va[cols, :] + 0.05 * g * g
-        u = m / (jnp.sqrt(v) + 1e-06) + 0.1 * w
+        m = mo[cols, :] + 0.1 * g
+        v = va[cols, :] + 0.05 * g * g
+        u = m / (jnp.sqrt(v) + 1e-06) + up[cols, :]
         mo[cols, :] = m
         va[cols, :] = v
         up[cols, :] = u
         u_sum += fold(u * u)
-        w_sum += fold(w * w)
     one[0, 0:4] = u_sum
     one[0, 4:8] = w_sum
     for px, pc, slot in group1:

time: 121 us -> 121 us (level)
  no operation moved by 1% of the time
where the time goes in v5:
time: 121 us; the launch traced here: 120 us
  Pallas kernels  120 us (99%)
    pallas_call x1, Pallas kernels, shards(): pl.pallas_call(functools.partial(kernel, multiplier), out_shape=(pltpu.VM...  118 us

profile of v5, /device:TPU:1, one launch (start us, length us, event | category | flops | bytes accessed | tf_op | source)
XLA Modules:
  0.0 120.5 jit_solution(337180324289291933)
XLA Ops:
  0.6 117.5 %step.1 = (bf16[1024,768]{1,0:T(8,128)(2,1)S(1)}, f32[384,768]{1,0:T(8,128)S(1)}, f32[384,768]{1,0:T(8,128)S(1)}, f32[384,768]{1,0:T(8,128)S(1)}, f32[8,128]{1,0:T(8,128)S(1)}) custom-call(bf16[128,6144]{1,0:T(8,128)(2,1)} %cot.1, bf16[1024,768]{1,0:T(8,128)(2,1)} %ctx.1, bf16[6144,768]{1,0:T(8,128)(2,1)} %weight.1, f32[384,768]{1,0:T(8,128)} %first.1, ...), custom_call_target="tpu_custom_call" | custom-call | flops 19327352832 | bytes 41943040 | tf_op jit(solution)/shard_map/step/pallas_call | solution.py:472
  118.2 2.3 %finish.1 = (bf16[1024,768]{1,0:T(8,128)(2,1)}, f32[384,768]{1,0:T(8,128)}, f32[384,768]{1,0:T(8,128)}, f32[384,768]{1,0:T(8,128)}) custom-call(bf16[1024,768]{1,0:T(8,128)(2,1)S(1)} %get-tuple-element.9.cg, f32[384,768]{1,0:T(8,128)S(1)} %get-tuple-element.10.mo, f32[384,768]{1,0:T(8,128)S(1)} %get-tuple-element.11.va, ...), custom_call_target="tpu_custom_call" | custom-call | tf_op jit(solution)/shard_map/finish/pallas_call | solution.py:488
